TPU v7x, 256 devices: a whole 4x4x8 slice. The times are simulated.
256 devices in a mesh: dp: 4 (over y), seq: 64 (over x, z, core).
Axes of the slice: x: 4, y: 4, z: 8, core: 2. Of those that a mesh axis runs over, the one named last changes fastest.
Arguments:
- hidden_in: bfloat16 [65536, 2048], P(('dp', 'seq')), parts along dimension 0, may hold values from -6 to 6
- lin_query: bfloat16 [65536, 1024], P(('dp', 'seq')), parts along dimension 0, may hold values from -6 to 6
- lin_key: bfloat16 [65536, 256], P(('dp', 'seq')), parts along dimension 0, may hold values from -6 to 6
- lin_value: bfloat16 [65536, 256], P(('dp', 'seq')), parts along dimension 0, may hold values from -6 to 6
- lin_gain: float32 [1024], replicated, may hold values from 0.1 to 1.9
- lin_out_weight: bfloat16 [1024, 2048], replicated, may hold values from -0.1875 to 0.1875
- soft_gain: float32 [2048], replicated, may hold values from 0.1 to 1.9
- soft_wq: bfloat16 [2048, 1024], replicated, may hold values from -4 to 4
- soft_wk: bfloat16 [2048, 256], replicated, may hold values from -4 to 4
- soft_wv: bfloat16 [2048, 256], replicated, may hold values from -0.125 to 0.125
- pattern: int32 [2, 128, 18], replicated, may hold values from 0 to 127, as said below
Outputs:
- attended: bfloat16 [65536, 1024], P(('dp', 'seq')), parts along dimension 0
There are 4 independent parts, one for each index of `dp`. A program takes and returns all parts, laid end to end along the dimension named above; an argument that names none is the same for every part. Nothing has to cross between parts.
Inputs may be any that keep to these rules, and one draw needn't show every extreme that they name: pattern[g, b, 0] = b and pattern[g, b, 1] = max(b - 1, 0); every entry of row b lies between 0 and b; for each key-value head and the 2 query blocks held by one device, the entries in slots 2 to 17 of those rows that lie in another device's tokens all name the same key block of that device.
All inputs are finite; a program needn't handle non-finite values.
Results may differ from a plain program's by a relative error of at most 0.035.
Values may be sent and summed in bfloat16 or wider, within the bound.
A program may use at most 128 MiB of HBM per device.

v0:
```python
import jax
import jax.numpy as jnp
from jax import lax
from jax.sharding import PartitionSpec as P

HEAD_DIM = 128
HEADS = 8
KV_HEADS = 2
BLOCK = 128
EPSILON = 1e-06


def carried_in(shard, axis, combine, identity):
    devices, position = (lax.axis_size(axis), lax.axis_index(axis))
    everything = lax.all_gather(shard, axis)
    start = jnp.broadcast_to(jnp.asarray(identity, shard.dtype), shard.shape)

    def lap(k, before):
        reached = k < position
        new = combine(before, everything[k])
        return jnp.where(reached, new, before)

    return lax.fori_loop(0, devices, lap, start)


def add_states(earlier, later):
    return earlier + later


def local(
    hidden_in,
    lin_query,
    lin_key,
    lin_value,
    lin_gain,
    lin_out_weight,
    soft_gain,
    soft_wq,
    soft_wk,
    soft_wv,
    pattern,
):
    tok_count = hidden_in.shape[0]
    local_blocks = tok_count // BLOCK
    per_group = HEADS // KV_HEADS
    listed = pattern.shape[2]
    position = lax.axis_index("seq")
    query_blocks = lin_query.reshape(local_blocks, BLOCK, KV_HEADS, per_group, HEAD_DIM)
    key_blocks = lin_key.reshape(local_blocks, BLOCK, KV_HEADS, HEAD_DIM)
    value_blocks = lin_value.reshape(local_blocks, BLOCK, KV_HEADS, HEAD_DIM)
    block_states = jnp.einsum(
        "ntgd,ntge->ngde", key_blocks, value_blocks, preferred_element_type=jnp.float32
    )
    device_state = jnp.sum(block_states, axis=0)
    carried = carried_in(device_state, "seq", add_states, jnp.zeros_like(device_state))
    running = jnp.concatenate(
        [jnp.zeros_like(block_states[:1]), jnp.cumsum(block_states[:-1], axis=0)], axis=0
    )
    before = carried[None] + running
    inter = jnp.einsum(
        "ntgpd,ngde->ntgpe",
        query_blocks.astype(jnp.float32),
        before,
        precision=lax.Precision.HIGHEST,
    )
    rows_here = jnp.arange(BLOCK)
    causal = rows_here[:, None] >= rows_here[None, :]
    local_scores = jnp.einsum(
        "ntgpd,nsgd->ngpts", query_blocks, key_blocks, preferred_element_type=jnp.float32
    )
    local_scores = jnp.where(causal, local_scores, 0.0).astype(jnp.bfloat16)
    intra = jnp.einsum(
        "ngpts,nsge->ntgpe", local_scores, value_blocks, preferred_element_type=jnp.float32
    )
    mixed = (inter + intra).reshape(tok_count, HEADS, HEAD_DIM)
    normed = (
        mixed
        * lax.rsqrt(jnp.mean(mixed * mixed, axis=-1, keepdims=True) + EPSILON)
        * lin_gain.reshape(HEADS, HEAD_DIM)
    )
    normed = normed.reshape(tok_count, HEADS * HEAD_DIM).astype(jnp.bfloat16)
    branch = jnp.dot(normed, lin_out_weight, preferred_element_type=jnp.float32)
    residual = (hidden_in.astype(jnp.float32) + branch).astype(jnp.bfloat16)
    widened = residual.astype(jnp.float32)
    layer_in = (
        widened
        * lax.rsqrt(jnp.mean(widened * widened, axis=-1, keepdims=True) + EPSILON)
        * soft_gain
    ).astype(jnp.bfloat16)
    soft_query = jnp.dot(layer_in, soft_wq, preferred_element_type=jnp.float32).astype(jnp.bfloat16)
    soft_key = jnp.dot(layer_in, soft_wk, preferred_element_type=jnp.float32).astype(jnp.bfloat16)
    soft_value = jnp.dot(layer_in, soft_wv, preferred_element_type=jnp.float32).astype(jnp.bfloat16)
    packed = jnp.concatenate(
        [
            soft_key.reshape(tok_count, KV_HEADS, HEAD_DIM),
            soft_value.reshape(tok_count, KV_HEADS, HEAD_DIM),
        ],
        axis=-1,
    )
    mine = lax.dynamic_slice_in_dim(pattern, position * local_blocks, local_blocks, 1)
    whole = lax.all_gather(packed, "seq", axis=0, tiled=True)
    table = whole.reshape(-1, BLOCK, KV_HEADS, 2 * HEAD_DIM)
    group_ids = jnp.arange(KV_HEADS)[:, None, None]
    tiles = table[mine, :, group_ids, :]
    tiles = tiles.reshape(KV_HEADS, local_blocks, listed * BLOCK, 2 * HEAD_DIM)
    keys_tile = tiles[..., :HEAD_DIM]
    values_tile = tiles[..., HEAD_DIM:]
    soft_blocks = soft_query.reshape(local_blocks, BLOCK, KV_HEADS, per_group, HEAD_DIM)
    scores = jnp.einsum(
        "ntgpd,gnkd->gnptk", soft_blocks, keys_tile, preferred_element_type=jnp.float32
    ) * HEAD_DIM ** (-0.5)
    same = mine[..., :, None] == mine[..., None, :]
    earlier = jnp.arange(listed)[None, :] < jnp.arange(listed)[:, None]
    repeated = jnp.any(same & earlier, axis=-1)
    live = jnp.repeat(jnp.logical_not(repeated), BLOCK, axis=-1)
    columns = jnp.arange(listed * BLOCK)
    causal_keys = (columns[None, :] >= BLOCK) | (columns[None, :] <= rows_here[:, None])
    allowed = live[:, :, None, None, :] & causal_keys[None, None, None]
    highest = jnp.max(jnp.where(allowed, scores, -jnp.inf), axis=-1, keepdims=True)
    weights = jnp.where(allowed, jnp.exp(scores - highest), 0.0)
    total = jnp.sum(weights, axis=-1, keepdims=True)
    probs = (weights / total).astype(jnp.bfloat16)
    attended = jnp.einsum(
        "gnptk,gnke->ntgpe", probs, values_tile, preferred_element_type=jnp.float32
    )
    return attended.reshape(tok_count, HEADS * HEAD_DIM).astype(jnp.bfloat16)


def solution(mesh):
    in_specs = (
        P(("dp", "seq"), None),
        P(("dp", "seq"), None),
        P(("dp", "seq"), None),
        P(("dp", "seq"), None),
        P(),
        P(),
        P(),
        P(),
        P(),
        P(),
        P(),
    )
    out_specs = P(("dp", "seq"), None)
    return jax.shard_map(local, mesh=mesh, in_specs=in_specs, out_specs=out_specs, check_vma=False)
```

profile of v0, /device:TPU:1, one launch (start us, length us, event | category | flops | bytes accessed | tf_op | source)
XLA Modules:
  0.0 329.4 jit_solution(11226672005344907080)
XLA Ops:
  6.5 1.0 reshape.120
  9.5 1.4 reshape.122
  10.9 86.4 %all-gather.6.cloned.1.call-done = f32[128,128,128]{2,1,0:T(8,128)} async-done(((f32[2,128,128]{2,1,0:T(8,128)}), f32[128,128,128]{2,1,0:T(8,128)}) %all-gather.6.cloned.1.call-update) | async-done | bytes 8388624 | tf_op jit(solution)/shard_map/all_gather | solution.py:15
  97.4 62.3 %while.14 = (s32[]{:T(128)}, f32[2,128,128]{2,1,0:T(8,128)S(1)}, s32[]{:T(128)}, f32[64,2,128,128]{3,2,1,0:T(8,128)}, s32[]{:T(128)}, /*index=5*/s32[]{:T(128)}) while((s32[]{:T(128)}, f32[2,128,128]{2,1,0:T(8,128)S(1)}, s32[]{:T(128)}, f32[64,2,128,128]{3,2,1,0:T(8,128)}, s32[]{:T(128)}, /*index=5*/s32[]{:T(128)}) %tuple.44), condition=%wide.region_2.3_spmd.clone, body=%wide.region_1.2_spmd.clone.sunk | while | flops 98308 | bytes 393317 | solution.py:23
  98.4 0.9 add_select_fusion.2
  99.3 0.9 add_select_fusion.2
  100.3 0.9 add_select_fusion.2
  101.3 0.9 add_select_fusion.2
  102.2 0.9 add_select_fusion.2
  103.2 0.9 add_select_fusion.2
  104.2 0.9 add_select_fusion.2
  105.2 0.9 add_select_fusion.2
  106.1 0.9 add_select_fusion.2
  107.1 0.9 add_select_fusion.2
  108.1 0.9 add_select_fusion.2
  109.1 0.9 add_select_fusion.2
  110.0 0.9 add_select_fusion.2
  111.0 0.9 add_select_fusion.2
  112.0 0.9 add_select_fusion.2
  113.0 0.9 add_select_fusion.2
  113.9 0.9 add_select_fusion.2
  114.9 0.9 add_select_fusion.2
  115.9 0.9 add_select_fusion.2
  116.9 0.9 add_select_fusion.2
  117.8 0.9 add_select_fusion.2
  118.8 0.9 add_select_fusion.2
  119.8 0.9 add_select_fusion.2
  120.7 0.9 add_select_fusion.2
  121.7 0.9 add_select_fusion.2
  122.7 0.9 add_select_fusion.2
  123.7 0.9 add_select_fusion.2
  124.6 0.9 add_select_fusion.2
  125.6 0.9 add_select_fusion.2
  126.6 0.9 add_select_fusion.2
  160.3 1.5 multiply_reduce_fusion
  161.9 1.7 copy.85
  164.4 3.9 %fusion.13 = (f32[256]{0:T(256)S(1)}, bf16[256,2048]{1,0:T(8,128)(2,1)S(1)}) fusion(bf16[1024,2048]{1,0:T(8,128)(2,1)} %param.18, f32[256,1024]{1,0:T(8,128)S(1)} %reshape.123, f32[32,8,8,128]{3,2,1,0:T(8,128)S(1)} %bitcast.81, f32[1024]{0:T(1024)S(1)} %copy-done.4, bf16[256,2048]{1,0:T(8,128)(2,1)} %param.13), kind=kOutput, calls=%fused_computation.24 | convolution fusion | flops 1077673728 | bytes 8393728 | tf_op jit(solution)/shard_map/dot_general | solution.py:82
  169.4 2.2 convolution_convert_fusion.2
  173.3 1.2 fusion.29
  174.5 1.7 broadcast_and_fusion
  176.3 3.8 %convolution_convert_fusion = bf16[256,1024]{1,0:T(8,128)(2,1)S(1)} fusion(bf16[2048,1024]{1,0:T(8,128)(2,1)} %param.20, bf16[256,2048]{1,0:T(8,128)(2,1)} %copy-done.5, f32[2048]{0:T(1024)S(1)} %copy-done.3, f32[256]{0:T(256)S(1)} %add_rsqrt_fusion.1), kind=kOutput, calls=%fused_computation.34 | convolution fusion | flops 1076101120 | bytes 5776384 | tf_op jit(solution)/shard_map/dot_general | solution.py:90
  180.4 89.2 %all-gather.4.cloned.1.call-done = bf16[16384,2,256]{2,0,1:T(8,128)(2,1)} async-done(((bf16[256,2,256]{2,0,1:T(8,128)(2,1)}), bf16[16384,2,256]{2,0,1:T(8,128)(2,1)}) %all-gather.4.cloned.1.call-update) | async-done | bytes 16777232 | tf_op jit(solution)/shard_map/all_gather | solution.py:101
  269.6 14.0 %copy.90 = bf16[128,128,2,256]{3,1,2,0:T(8,128)(2,1)} copy(bf16[128,128,2,256]{3,1,0,2:T(8,128)(2,1)} %bitcast.76) | data formatting | bytes 33554432 | tf_op jit(solution)/shard_map/reshape | solution.py:102
  283.6 12.9 %gather_fusion = bf16[72,128,256]{2,1,0:T(8,128)(2,1)} fusion(bf16[128,128,2,256]{3,1,2,0:T(8,128)(2,1)} %copy.90, s32[72]{0:T(128)S(1)} %reshape.129), kind=kCustom, calls=%fused_computation | custom fusion | bytes 9437760 | tf_op jit(solution)/shard_map/gather | solution.py:104
  296.5 4.3 %fusion.11 = f32[2,2,2304,128,4]{3,2,4,1,0:T(8,128)S(1)} fusion(bf16[2,2,2304,256]{3,2,1,0:T(8,128)(2,1)} %bitcast.77, bf16[2,128,2,4,128]{4,3,2,1,0:T(4,128)(2,1)S(1)} %reshape.128), kind=kOutput, calls=%fused_computation.20 | convolution fusion | flops 1207959552 | bytes 21757952 | tf_op jit(solution)/shard_map/ntgpd,gnkd->gnptk/dot_general | solution.py:109
  300.8 11.6 %fusion.64 = (f32[2,2,4,128]{3,2,1,0:T(4,128)S(1)}, f32[2,2,4,128,2304]{3,4,2,1,0:T(8,128)}) fusion(f32[2,2,2304,128,4]{3,2,4,1,0:T(8,128)S(1)} %fusion.11, pred[2,2,128,2304]{2,3,1,0:T(8,128)(4,1)S(1)} %broadcast_and_fusion), kind=kOutput, calls=%fused_computation.76 | output fusion | flops 28313856 | bytes 38936576 | tf_op jit(solution)/shard_map/sub | solution.py:120
  312.3 8.8 %fusion.24 = bf16[2,128,2,4,128]{1,4,3,2,0:T(8,128)(2,1)S(1)} fusion(f32[2,2,4,128,2304]{3,4,2,1,0:T(8,128)} %get-tuple-element.117, f32[2,2,4,128]{3,2,1,0:T(4,128)S(1)} %get-tuple-element.116, bf16[2,2,2304,256]{3,2,1,0:T(8,128)(2,1)} %bitcast.78), kind=kOutput, calls=%fused_computation.35 | convolution fusion | flops 1217658880 | bytes 21766144 | tf_op jit(solution)/shard_map/gnptk,gnke->ntgpe/dot_general | solution.py:123
  321.4 1.2 convert_element_type.52
  (78 shorter events, 39.1 us)
Async XLA Ops:
  6.5 161.8 %copy-start = (bf16[2048,256]{1,0:T(8,128)(2,1)S(1)}, bf16[2048,256]{1,0:T(8,128)(2,1)}, u32[]{:S(2)}) copy-start(bf16[2048,256]{1,0:T(8,128)(2,1)} %param.22) | copy-start | bytes 3145732
  6.5 90.8 %all-gather.6.cloned.1.call-start = ((), (), s32[]{:S(2)}) async-start(), calls=%async_computation.1 | async-start | bytes 8519680 | tf_op jit(solution)/shard_map/all_gather | solution.py:15
  9.4 260.2 %all-gather.4.cloned.1.call-start = ((), (), s32[]{:S(2)}) async-start(), calls=%async_computation | async-start | bytes 17039360 | tf_op jit(solution)/shard_map/all_gather | solution.py:101
  159.7 4.7 %copy-start.4 = (f32[1024]{0:T(1024)S(1)}, f32[1024]{0:T(1024)}, u32[]{:S(2)}) copy-start(f32[1024]{0:T(1024)} %param.17) | copy-start | bytes 12292
  164.4 4.0 %copy-start.3 = (f32[2048]{0:T(1024)S(1)}, f32[2048]{0:T(1024)}, u32[]{:S(2)}) copy-start(f32[2048]{0:T(1024)} %param.19) | copy-start | bytes 24580
  168.3 1.0 copy-start.5
  168.3 4.2 %copy-start.2 = (s32[2,128,18]{1,0,2:T(2,128)S(1)}, s32[2,128,18]{1,0,2:T(2,128)}, u32[]{:S(2)}) copy-start(s32[2,128,18]{1,0,2:T(2,128)} %param.23) | copy-start | bytes 55300
  312.3 10.3 %copy-start.1 = (bf16[2048,256]{1,0:T(8,128)(2,1)S(1)}, bf16[2048,256]{1,0:T(8,128)(2,1)}, u32[]{:S(2)}) copy-start(bf16[2048,256]{1,0:T(8,128)(2,1)} %param.22) | copy-start | bytes 3145732
Sparse Core Ops, SparseCore 0:
  10.1 87.1 all-gather.5
  172.6 96.9 all-gather.3
where the time goes:
time: 331 us; the launch traced here: 329 us
  waiting for transfers between devices  176 us (53%)
  other arithmetic  76.4 us (23%)
  local copies, waits for them, and re-layouts  35.5 us (11%)
  matrix products  26.7 us (8%)
  between operations  13.7 us (4%)
    all_gather x1, waiting for transfers between devices, local(): whole = lax.all_gather(packed, 'seq', axis=0, tiled=True)  89.2 us
    all_gather x1, waiting for transfers between devices, carried_in(): everything = lax.all_gather(shard, axis)  86.4 us
    select_n x64, other arithmetic, lap(): return jnp.where(reached, new, before)  60.8 us
    reshape x1, local copies, waits for them, and re-layouts, local(): table = whole.reshape(-1, BLOCK, KV_HEADS, 2 * HEAD_DIM)  14 us
    gather x1, local copies, waits for them, and re-layouts, local(): tiles = table[mine, :, group_ids, :]  12.9 us
    sub x1, other arithmetic, local(): weights = jnp.where(allowed, jnp.exp(scores - highest), 0.0)  11.6 us
    dot_general x1, matrix products, local(): jnp.einsum('gnptk,gnke->ntgpe', probs, values_tile, preferred_element_typ...  8.79 us
  transfers between devices with their start and end apart: 2, of which 2 were waited for; matrix products, arithmetic and copies ran while one was open for 3% of the time, Pallas kernels for 0%

commit v1 on v0

--- a/solution.py
+++ b/solution.py
@@ -98,7 +98,9 @@
         axis=-1,
     )
     mine = lax.dynamic_slice_in_dim(pattern, position * local_blocks, local_blocks, 1)
-    whole = lax.all_gather(packed, "seq", axis=0, tiled=True)
+    whole = jnp.concatenate(
+        lax.all_to_all(jnp.stack([packed] * lax.axis_size("seq")), "seq", 0, 0), axis=0
+    )
     table = whole.reshape(-1, BLOCK, KV_HEADS, 2 * HEAD_DIM)
     group_ids = jnp.arange(KV_HEADS)[:, None, None]
     tiles = table[mine, :, group_ids, :]

time: 331 us -> 611 us (1.85)
  waiting for transfers between devices: 176 us -> 444 us
  local copies, waits for them, and re-layouts: 35.5 us -> 42.3 us
  starting transfers between devices: 0.04 us -> 6.57 us
    all_to_all x0 -> x1, waiting for transfers between devices: none -> 358 us  [local(): lax.all_to_all(jnp.stack([packed] * lax.axis_size('seq')), 'seq', 0, 0)]
    all_gather x1 -> x0, waiting for transfers between devices: 89.2 us -> none  [local(): whole = lax.all_gather(packed, 'seq', axis=0, tiled=True)]
    reshape x3 -> x0, local copies, waits for them, and re-layouts: 14.2 us -> none  [the longest x1 14 us: local(): table = whole.reshape(-1, BLOCK, KV_HEADS, 2 * HEAD_DIM)]
    another operation x0 -> x2, local copies, waits for them, and re-layouts: none -> 12.6 us  [the longest x1 6.58 us: local(): table = whole.reshape(-1, BLOCK, KV_HEADS, 2 * HEAD_DIM)]
    all_to_all x0 -> x1, local copies, waits for them, and re-layouts: none -> 8.6 us  [local(): lax.all_to_all(jnp.stack([packed] * lax.axis_size('seq')), 'seq', 0, 0)]
    all_to_all x0 -> x1, starting transfers between devices: none -> 6.57 us  [local(): lax.all_to_all(jnp.stack([packed] * lax.axis_size('seq')), 'seq', 0, 0)]
  transfers between devices with their start and end apart: 2 -> 2, of which waited for: 2 -> 2; matrix products, arithmetic and copies ran while one was open for 3% -> 2% of each run, Pallas kernels for 0% -> 0%
where the time goes in v1:
time: 611 us; the launch traced here: 609 us
  waiting for transfers between devices  444 us (73%)
  other arithmetic  75.8 us (12%)
  local copies, waits for them, and re-layouts  42.3 us (7%)
  matrix products  25.2 us (4%)
  between operations  13.7 us (2%)
  starting transfers between devices  6.57 us (1%)
    all_to_all x1, waiting for transfers between devices, local(): lax.all_to_all(jnp.stack([packed] * lax.axis_size('seq')), 'seq', 0, 0)  358 us
    all_gather x1, waiting for transfers between devices, carried_in(): everything = lax.all_gather(shard, axis)  86.5 us
    select_n x64, other arithmetic, lap(): return jnp.where(reached, new, before)  60.9 us
    gather x1, local copies, waits for them, and re-layouts, local(): tiles = table[mine, :, group_ids, :]  12.8 us
  transfers between devices with their start and end apart: 2, of which 2 were waited for; matrix products, arithmetic and copies ran while one was open for 2% of the time, Pallas kernels for 0%

profile of v1, /device:TPU:1, one launch (start us, length us, event | category | flops | bytes accessed | tf_op | source)
XLA Modules:
  0.0 609.2 jit_solution(4661039865929463582)
XLA Ops:
  6.5 1.0 reshape.119
  9.5 1.4 reshape.121
  10.9 86.5 %all-gather.3.cloned.1.call-done = f32[128,128,128]{2,1,0:T(8,128)} async-done(((f32[2,128,128]{2,1,0:T(8,128)}), f32[128,128,128]{2,1,0:T(8,128)}) %all-gather.3.cloned.1.call-update) | async-done | bytes 8388624 | tf_op jit(solution)/shard_map/all_gather | solution.py:15
  97.4 62.4 %while.14 = (s32[]{:T(128)}, f32[2,128,128]{2,1,0:T(8,128)S(1)}, s32[]{:T(128)}, f32[64,2,128,128]{3,2,1,0:T(8,128)}, s32[]{:T(128)}, /*index=5*/s32[]{:T(128)}) while((s32[]{:T(128)}, f32[2,128,128]{2,1,0:T(8,128)S(1)}, s32[]{:T(128)}, f32[64,2,128,128]{3,2,1,0:T(8,128)}, s32[]{:T(128)}, /*index=5*/s32[]{:T(128)}) %tuple.42), condition=%wide.region_2.3_spmd.clone, body=%wide.region_1.2_spmd.clone.sunk | while | flops 98308 | bytes 393317 | solution.py:23
  98.4 1.0 add_select_fusion.2
  99.3 1.0 add_select_fusion.2
  100.3 1.0 add_select_fusion.2
  101.3 1.0 add_select_fusion.2
  102.3 1.0 add_select_fusion.2
  103.2 1.0 add_select_fusion.2
  104.2 1.0 add_select_fusion.2
  105.2 1.0 add_select_fusion.2
  106.2 1.0 add_select_fusion.2
  107.1 1.0 add_select_fusion.2
  108.1 1.0 add_select_fusion.2
  109.1 1.0 add_select_fusion.2
  110.1 1.0 add_select_fusion.2
  111.0 1.0 add_select_fusion.2
  112.0 1.0 add_select_fusion.2
  113.0 1.0 add_select_fusion.2
  114.0 1.0 add_select_fusion.2
  114.9 1.0 add_select_fusion.2
  125.7 1.0 add_select_fusion.2
  127.6 1.0 add_select_fusion.2
  129.6 1.0 add_select_fusion.2
  131.5 1.0 add_select_fusion.2
  133.5 1.0 add_select_fusion.2
  144.2 1.0 add_select_fusion.2
  146.2 1.0 add_select_fusion.2
  148.1 1.0 add_select_fusion.2
  150.1 1.0 add_select_fusion.2
  152.0 1.0 add_select_fusion.2
  160.4 1.5 multiply_reduce_fusion
  162.1 1.7 copy.86
  164.5 4.0 fusion.13
  170.1 6.1 stack.2
  176.2 6.6 %all-to-all-start = ((bf16[64,256,2,256]{3,1,2,0:T(8,128)(2,1)}), bf16[64,256,2,256]{3,1,2,0:T(8,128)(2,1)}, u32[]{:S(2)}, u32[]{:S(2)}) async-start(bf16[64,256,2,256]{3,1,2,0:T(8,128)(2,1)} %stack.2), calls=%async_computation | async-start | bytes 33554432 | tf_op jit(solution)/shard_map/all_to_all | solution.py:102
  183.6 1.2 fusion.29
  184.8 1.7 broadcast_and_fusion
  186.5 3.8 convolution_convert_fusion
  190.7 357.6 %all-to-all-done = bf16[64,256,2,256]{3,1,2,0:T(8,128)(2,1)} async-done(((bf16[64,256,2,256]{3,1,2,0:T(8,128)(2,1)}), bf16[64,256,2,256]{3,1,2,0:T(8,128)(2,1)}, u32[]{:S(2)}, u32[]{:S(2)}) %all-to-all-start) | async-done | bytes 16777248 | tf_op jit(solution)/shard_map/all_to_all | solution.py:102
  548.3 8.6 %copy.89 = bf16[64,256,2,256]{3,1,0,2:T(8,128)(2,1)S(1)} copy(bf16[64,256,2,256]{3,1,2,0:T(8,128)(2,1)} %all-to-all-done) | data formatting | bytes 33554432 | tf_op jit(solution)/shard_map/all_to_all | solution.py:102
  556.9 6.6 %copy.91 = bf16[128,128,2,256]{3,1,2,0:T(8,128)(2,1)} copy(bf16[128,128,2,256]{3,1,0,2:T(8,128)(2,1)S(1)} %bitcast.76) | data formatting | bytes 33554432 | tf_op jit(solution)/shard_map/reshape;reshape | solution.py:104
  563.5 12.8 %gather_fusion = bf16[72,128,256]{2,1,0:T(8,128)(2,1)} fusion(bf16[128,128,2,256]{3,1,2,0:T(8,128)(2,1)} %copy.91, s32[72]{0:T(128)S(1)} %reshape.127), kind=kCustom, calls=%fused_computation | custom fusion | bytes 9437760 | tf_op jit(solution)/shard_map/gather | solution.py:106
  576.3 4.3 fusion.11
  580.5 11.5 %fusion.64 = (f32[2,2,4,128]{3,2,1,0:T(4,128)S(1)}, f32[2,2,4,128,2304]{3,4,2,1,0:T(8,128)}) fusion(f32[2,2,2304,128,4]{3,2,4,1,0:T(8,128)S(1)} %fusion.11, pred[2,2,128,2304]{2,3,1,0:T(8,128)(4,1)S(1)} %broadcast_and_fusion), kind=kOutput, calls=%fused_computation.76 | output fusion | flops 28313856 | bytes 38936576 | tf_op jit(solution)/shard_map/sub | solution.py:122
  592.1 8.8 %fusion.24 = bf16[2,128,2,4,128]{1,4,3,2,0:T(8,128)(2,1)S(1)} fusion(f32[2,2,4,128,2304]{3,4,2,1,0:T(8,128)} %get-tuple-element.117, f32[2,2,4,128]{3,2,1,0:T(4,128)S(1)} %get-tuple-element.116, bf16[2,2,2304,256]{3,2,1,0:T(8,128)(2,1)} %bitcast.78), kind=kOutput, calls=%fused_computation.35 | convolution fusion | flops 1217658880 | bytes 21766144 | tf_op jit(solution)/shard_map/gnptk,gnke->ntgpe/dot_general | solution.py:125
  601.2 1.2 convert_element_type.52
  (80 shorter events, 40.6 us)
Async XLA Ops:
  6.5 162.0 %copy-start = (bf16[2048,256]{1,0:T(8,128)(2,1)S(1)}, bf16[2048,256]{1,0:T(8,128)(2,1)}, u32[]{:S(2)}) copy-start(bf16[2048,256]{1,0:T(8,128)(2,1)} %param.22) | copy-start | bytes 3145732
  6.5 90.8 %all-gather.3.cloned.1.call-start = ((), (), s32[]{:S(2)}) async-start(), calls=%async_computation.1 | async-start | bytes 8519680 | tf_op jit(solution)/shard_map/all_gather | solution.py:15
  159.8 4.7 copy-start.5
  164.5 4.1 copy-start.4
  164.5 4.7 copy-start.3
  168.5 1.4 copy-start.6
  176.2 6.6 %copy-start.2 = (s32[2,128,18]{1,0,2:T(2,128)S(1)}, s32[2,128,18]{1,0,2:T(2,128)}, u32[]{:S(2)}) copy-start(s32[2,128,18]{1,0,2:T(2,128)} %param.23) | copy-start | bytes 55300
  176.2 372.1 %all-to-all-start = ((bf16[64,256,2,256]{3,1,2,0:T(8,128)(2,1)}), bf16[64,256,2,256]{3,1,2,0:T(8,128)(2,1)}, u32[]{:S(2)}, u32[]{:S(2)}) async-start(bf16[64,256,2,256]{3,1,2,0:T(8,128)(2,1)} %stack.2), calls=%async_computation | async-start | bytes 33554432 | tf_op jit(solution)/shard_map/all_to_all | solution.py:102
  592.1 10.3 %copy-start.1 = (bf16[2048,256]{1,0:T(8,128)(2,1)S(1)}, bf16[2048,256]{1,0:T(8,128)(2,1)}, u32[]{:S(2)}) copy-start(bf16[2048,256]{1,0:T(8,128)(2,1)} %param.22) | copy-start | bytes 3145732
Sparse Core Ops, SparseCore 0:
  10.1 87.1 all-gather.2
